TPU v7x, 256 devices: a whole 4x4x8 slice. The times are simulated.
256 devices in a mesh: row: 8 (over z_hi, x), col: 32 (over z_lo, y, core).
Axes of the slice: x: 4, y: 4, z: 8 (z_hi: 2, z_lo: 4; z = z_hi * 4 + z_lo), core: 2. Of those that a mesh axis runs over, the one named last changes fastest.
Arguments:
- pair: float32 [512, 512, 128], P('row', 'col'), may hold values from -6 to 6
- pair_mask: int32 [512, 512], P('row', 'col'), may hold values 0 or 1
- norm_gain: float32 [128], replicated, may hold values from 0.1 to 1.9
- left_weight: bfloat16 [128, 256], replicated, may hold values from -0.5 to 0.5
- right_weight: bfloat16 [128, 256], replicated, may hold values from -0.5 to 0.5
- gate_weight: bfloat16 [128, 128], replicated, may hold values from -0.5 to 0.5
- out_gain: float32 [128], replicated, may hold values from 0.1 to 1.9
- out_weight: bfloat16 [128, 128], replicated, may hold values from -0.5 to 0.5
Outputs:
- update: bfloat16 [512, 512, 128], P('row', 'col')
All inputs are finite; a program needn't handle non-finite values. No bound on the sum of `pair_mask` on one device may be relied on, other than what follows from the above.
Results may differ from a plain program's by a relative error of at most 0.0078.
Values may be sent and summed in bfloat16 or wider, within the bound.
A program may use at most 128 MiB of HBM per device.

v0:
```python
import jax
import jax.numpy as jnp
from jax import lax
from jax.sharding import PartitionSpec as P


def from_root(shard, axis, root):
    mine = lax.axis_index(axis) == root
    return lax.psum(jnp.where(mine, shard, jnp.zeros_like(shard)), axis)


def layer_norm(values, gain):
    mean = jnp.mean(values, axis=-1, keepdims=True)
    centered = values - mean
    spread = jnp.mean(centered * centered, axis=-1, keepdims=True)
    return centered * lax.rsqrt(spread + 1e-05) * gain


def edges(normed, weight, mask_f):
    hidden = weight.shape[1] // 2
    proj = jnp.dot(normed, weight, preferred_element_type=jnp.float32)
    return (jax.nn.sigmoid(proj[..., :hidden]) * proj[..., hidden:] * mask_f).astype(jnp.bfloat16)


def body(pair, pair_mask, norm_gain, left_weight, right_weight, gate_weight, out_gain, out_weight):
    own_rows, own_cols = (pair.shape[0], pair.shape[1])
    normed = layer_norm(pair, norm_gain).astype(jnp.bfloat16)
    mask_f = pair_mask.astype(jnp.float32)[..., None]
    left = edges(normed, left_weight, mask_f)
    right = edges(normed, right_weight, mask_f)
    gate = jax.nn.sigmoid(jnp.dot(normed, gate_weight, preferred_element_type=jnp.float32))
    ratio = lax.axis_size("col") // lax.axis_size("row")
    col_index = lax.axis_index("col")
    slab = lax.all_gather(right, "col", axis=1, tiled=True)
    mirror = lax.dynamic_slice_in_dim(slab, col_index % ratio * own_cols, own_cols, 0)
    right_rows = from_root(mirror, "row", col_index // ratio)
    triangle = jnp.einsum(
        "ikh,jkh->ijh",
        lax.all_gather(left, "col", axis=1, tiled=True),
        right_rows,
        preferred_element_type=jnp.float32,
    )
    tri_normed = layer_norm(triangle, out_gain).astype(jnp.bfloat16)
    update = gate * jnp.dot(tri_normed, out_weight, preferred_element_type=jnp.float32)
    return update.astype(jnp.bfloat16)


def solution(mesh):
    in_specs = (P("row", "col", None), P("row", "col"), P(), P(), P(), P(), P(), P())
    out_specs = P("row", "col", None)
    return jax.shard_map(body, mesh=mesh, in_specs=in_specs, out_specs=out_specs, check_vma=False)
```

profile of v0, /device:TPU:1, one launch (start us, length us, event | category | flops | bytes accessed | tf_op | source)
XLA Modules:
  0.0 345.9 jit_solution(4468492165127698794)
XLA Ops:
  6.5 1.3 reduce_sum.36
  7.8 0.1 copy.29
  7.9 0.1 copy.30
  8.0 1.4 multiply_reduce_fusion.1
  9.5 0.1 copy.32
  9.6 1.4 multiply_convert_fusion.1
  11.0 0.3 fusion.14
  11.3 0.3 fusion.16
  11.6 0.1 copy.33
  11.7 1.1 fusion.5
  12.8 0.7 all-gather.5.cloned.1.call-update
  13.6 91.0 %all-gather.3.cloned.1.call-done = bf16[64,512,128]{2,1,0:T(8,128)(2,1)} async-done(((bf16[64,16,128]{2,1,0:T(8,128)(2,1)}), bf16[64,512,128]{2,1,0:T(8,128)(2,1)}) %all-gather.3.cloned.1.call-update) | async-done | bytes 8388624 | tf_op jit(solution)/shard_map/all_gather | solution.py:34
  104.6 3.1 dynamic-slice_select_fusion
  107.8 0.7 copy-done.5
  108.5 0.3 fusion.2
  108.8 84.3 %all-gather.5.cloned.1.call-done = bf16[64,512,128]{2,1,0:T(8,128)(2,1)} async-done(((bf16[64,16,128]{2,1,0:T(8,128)(2,1)}), bf16[64,512,128]{2,1,0:T(8,128)(2,1)}) %all-gather.5.cloned.1.call-update) | async-done | bytes 8388624 | tf_op jit(solution)/shard_map/all_gather | solution.py:39
  193.1 29.2 %copy.35 = bf16[64,512,128]{0,1,2:T(8,128)(2,1)} copy(bf16[64,512,128]{2,1,0:T(8,128)(2,1)} %all-gather.5.cloned.1.call-done) | data formatting | bytes 16777216 | tf_op jit(solution)/shard_map/all_gather | solution.py:39
  222.3 104.6 %all-reduce.2.cloned.1.call-done = bf16[16,512,128]{2,1,0:T(8,128)(2,1)} async-done(((bf16[16,512,128]{2,1,0:T(8,128)(2,1)}), bf16[16,512,128]{2,1,0:T(8,128)(2,1)}) %all-reduce.2.cloned.1.call-update) | async-done | bytes 2097168 | tf_op jit(solution)/shard_map/psum | solution.py:9
  326.9 3.4 copy.34
  330.3 7.1 %fusion.20 = (f32[64,16]{0,1:T(8,128)S(1)}, f32[64,16,128]{0,1,2:T(8,128)S(1)}) fusion(bf16[16,512,128]{1,0,2:T(8,128)(2,1)S(1)} %copy.34, bf16[64,512,128]{0,1,2:T(8,128)(2,1)} %copy.35), kind=kOutput, calls=%fused_computation.36 | convolution fusion | flops 134347776 | bytes 11014144 | tf_op jit(solution)/shard_map/ikh,jkh->ijh/dot_general | solution.py:37
  337.4 0.2 multiply_reduce_fusion
  337.6 0.2 multiply_convert_fusion
  337.9 0.6 copy.36
  338.5 0.9 fusion.3
  (22 shorter events, 0.2 us)
Async XLA Ops:
  6.5 4.4 %copy-start = (bf16[128,256]{1,0:T(8,128)(2,1)S(1)}, bf16[128,256]{1,0:T(8,128)(2,1)}, u32[]{:S(2)}) copy-start(bf16[128,256]{1,0:T(8,128)(2,1)} %param.11) | copy-start | bytes 196612
  6.5 4.7 %copy-start.1 = (bf16[128,256]{1,0:T(8,128)(2,1)S(1)}, bf16[128,256]{1,0:T(8,128)(2,1)}, u32[]{:S(2)}) copy-start(bf16[128,256]{1,0:T(8,128)(2,1)} %param.12) | copy-start | bytes 196612
  6.5 98.1 %all-gather.3.cloned.1.call-start = ((), (), s32[]{:S(2)}) async-start(), calls=%async_computation | async-start | bytes 8650752 | tf_op jit(solution)/shard_map/all_gather | solution.py:34
  8.0 3.6 %copy-start.3 = (s32[64,16]{0,1:T(8,128)S(1)}, s32[64,16]{0,1:T(8,128)}, u32[]{:S(2)}) copy-start(s32[64,16]{0,1:T(8,128)} %param.9) | copy-start | bytes 12292
  12.8 180.3 %all-gather.5.cloned.1.call-start = ((), (), s32[]{:S(2)}) async-start(), calls=%async_computation.2 | async-start | bytes 8650752 | tf_op jit(solution)/shard_map/all_gather | solution.py:39
  13.6 313.3 %all-reduce.2.cloned.1.call-start = ((), (), s32[]{:S(2)}) async-start(), calls=%async_computation.1 | async-start | bytes 4194304 | tf_op jit(solution)/shard_map/psum | solution.py:9
  107.7 0.8 copy-start.5
  330.3 7.3 %copy-start.4 = (f32[128]{0:T(128)S(1)}, f32[128]{0:T(128)}, u32[]{:S(2)}) copy-start(f32[128]{0:T(128)} %param.14) | copy-start | bytes 1540
  337.4 1.1 copy-start.2
Sparse Core Ops, SparseCore 0:
  12.9 91.6 all-gather.2
  106.4 86.6 all-gather.4
  195.8 131.0 all-reduce.1
where the time goes:
time: 348 us; the launch traced here: 346 us
  waiting for transfers between devices  281 us (81%)
  local copies, waits for them, and re-layouts  34.3 us (10%)
  between operations  13.3 us (4%)
  matrix products  8.8 us (3%)
  other arithmetic  8.76 us (3%)
    psum x1, waiting for transfers between devices, from_root(): return lax.psum(jnp.where(mine, shard, jnp.zeros_like(shard)), axis)  105 us
    all_gather x1, waiting for transfers between devices, body(): slab = lax.all_gather(right, 'col', axis=1, tiled=True)  91 us
    all_gather x1, waiting for transfers between devices, body(): lax.all_gather(left, 'col', axis=1, tiled=True)  84.3 us
    all_gather x1, local copies, waits for them, and re-layouts, body(): lax.all_gather(left, 'col', axis=1, tiled=True)  29.2 us
    dot_general x1, matrix products, body(): jnp.einsum('ikh,jkh->ijh', lax.all_gather(left, 'col', axis=1, tiled=True...  7.06 us
  transfers between devices with their start and end apart: 3, of which 3 were waited for; matrix products, arithmetic and copies ran while one was open for 9% of the time, Pallas kernels for 0%

commit v1 on v0

v1 whole, which is shorter than its diff:
```python
import jax
import jax.numpy as jnp
from jax import lax
from jax.experimental import pallas as pl
from jax.experimental.pallas import tpu as pltpu
from jax.sharding import PartitionSpec as P

F32 = jnp.float32
BF16 = jnp.bfloat16
EPS = 1e-05
CHIPS = 128


def rem(a, b):
    return lax.rem(a, jnp.int32(b))


def div(a, b):
    return lax.div(a, jnp.int32(b))


def kernel(
    pair_ref, mask_ref, norm_gain_ref, left_w_ref, right_w_ref, gate_w_ref, out_gain_ref, out_w_ref,
    out_ref,
    gate, edges, packed, send, recv, part, other, osend, orecv, flat, rows_out,
    send_sem, recv_sem, osend_sem, orecv_sem, xsend_sem, xrecv_sem,
):
    row = lax.axis_index("row")
    col = lax.axis_index("col")
    core = rem(col, 2)
    x = rem(row, 4)
    y = rem(div(col, 2), 4)
    z = div(row, 4) * 4 + div(col, 8)
    me = row * 16 + div(col, 2)

    def peer(step):
        pz = rem(z + rem(step, 8), 8)
        py = rem(y + rem(div(step, 8), 4), 4)
        px = rem(x + div(step, 32), 4)
        prow = div(pz, 4) * 4 + px
        pchip = rem(pz, 4) * 4 + py
        return prow * 16 + pchip, prow, pchip * 2 + core

    partner = {"col": col + 1 - 2 * core}

    barrier = pltpu.get_barrier_semaphore()

    def greet(step, carry):
        _, prow, pcol = peer(step)
        pl.semaphore_signal(barrier, inc=1, device_id=(prow, pcol), device_id_type=pl.DeviceIdType.MESH)
        return carry

    lax.fori_loop(1, CHIPS, greet, 0)
    pl.semaphore_signal(barrier, inc=1, device_id=partner, device_id_type=pl.DeviceIdType.MESH)

    gain = norm_gain_ref[...]
    for block in range(4):
        values = pair_ref[pl.ds(block * 16, 16)].reshape(256, 128)
        mean = jnp.mean(values, axis=-1, keepdims=True)
        centered = values - mean
        spread = jnp.mean(centered * centered, axis=-1, keepdims=True)
        normed = (centered * lax.rsqrt(spread + EPS) * gain).astype(BF16)
        here = pl.ds(block * 256, 256)
        for side, weight in ((0, left_w_ref), (1, right_w_ref)):
            proj = jnp.dot(normed, weight[...], preferred_element_type=F32)
            edges[side, here, :] = jax.nn.sigmoid(proj[:, :128]) * proj[:, 128:]
        gate[here, :] = jax.nn.sigmoid(jnp.dot(normed, gate_w_ref[...], preferred_element_type=F32))

    odd = rem(row, 2)
    for k in range(16):
        first = edges[odd, pl.ds(k, 64, stride=16), :]
        second = edges[1 - odd, pl.ds(k, 64, stride=16), :]
        packed[pl.ds(k, 128, stride=16), :] = jnp.concatenate([first, second], axis=0).T
    mask = mask_ref[...].astype(F32)
    mask = jnp.concatenate([mask, mask], axis=0).T
    send[...] = (packed[...].reshape(128, 16, 128) * mask[None]).astype(BF16)

    pl.semaphore_wait(barrier, CHIPS)

    own = pltpu.make_async_copy(send.at[me], recv.at[me], recv_sem)
    own.start()

    def scatter(step, carry):
        there, prow, pcol = peer(step)
        pltpu.make_async_remote_copy(
            src_ref=send.at[there], dst_ref=recv.at[me], send_sem=send_sem, recv_sem=recv_sem,
            device_id=(prow, pcol), device_id_type=pl.DeviceIdType.MESH,
        ).start()
        return carry

    lax.fori_loop(1, CHIPS, scatter, 0)
    pltpu.make_async_copy(recv, recv, recv_sem).wait()

    low = lax.broadcasted_iota(jnp.int32, (256, 128), 1) < 64
    lefts, rights = [], []
    for pair_at in range(4):
        even = recv[pl.ds(pair_at * 32, 16)].reshape(256, 128)
        uneven = recv[pl.ds(pair_at * 32 + 16, 16)].reshape(256, 128)
        lefts.append(jnp.where(low, even, uneven))
        rights.append(jnp.where(low, uneven, even))
    left = jnp.concatenate(lefts, axis=1)
    for pair_at in range(4):
        products = lax.dot_general(
            rights[pair_at], left, (((0,), (0,)), ((), ())), preferred_element_type=F32
        )
        for half in range(2):
            r = pair_at * 2 + 1 - half
            for q in range(4):
                at = half * 64 + q * 16
                part[q % 2, pl.ds((r * 2 + q // 2) * 16, 16), :] = products[at:at + 16]

    swap = pltpu.make_async_remote_copy(
        src_ref=part.at[1 - core], dst_ref=other, send_sem=xsend_sem, recv_sem=xrecv_sem,
        device_id=partner, device_id_type=pl.DeviceIdType.MESH,
    )
    swap.start()
    pltpu.make_async_copy(send.at[pl.ds(0, CHIPS - 1)], send.at[pl.ds(0, CHIPS - 1)], send_sem).wait()
    swap.wait_recv()

    low8 = lax.broadcasted_iota(jnp.int32, (256 // 2, 128), 1) < 64
    for pair_at in range(4):
        lanes = pl.ds(pair_at * 128, 128)
        total = (part[core, :, lanes] + other[:, lanes]).reshape(16, 2, 8, 128)
        top = total[:, 0].reshape(128, 128)
        bottom = total[:, 1].reshape(128, 128)
        even = jnp.where(low8, top, pltpu.roll(bottom, 64, 1))
        uneven = jnp.where(low8, pltpu.roll(top, 64, 1), bottom)
        osend[pl.ds(pair_at * 32, 16)] = even.reshape(16, 8, 128).astype(BF16)
        osend[pl.ds(pair_at * 32 + 16, 16)] = uneven.reshape(16, 8, 128).astype(BF16)

    own_back = pltpu.make_async_copy(osend.at[me], orecv.at[me], orecv_sem)
    own_back.start()

    def give_back(step, carry):
        there, prow, pcol = peer(step)
        pltpu.make_async_remote_copy(
            src_ref=osend.at[there], dst_ref=orecv.at[me], send_sem=osend_sem, recv_sem=orecv_sem,
            device_id=(prow, pcol), device_id_type=pl.DeviceIdType.MESH,
        ).start()
        return carry

    lax.fori_loop(1, CHIPS, give_back, 0)
    swap.wait_send()
    pltpu.make_async_copy(orecv, orecv, orecv_sem).wait()

    tri = orecv[...].astype(F32)
    mean = jnp.sum(tri, axis=0, keepdims=True) * (1.0 / 128)
    centered = tri - mean
    spread = jnp.sum(centered * centered, axis=0, keepdims=True) * (1.0 / 128)
    flat[...] = (centered * lax.rsqrt(spread + EPS)).reshape(1024, 128)
    out_gain = out_gain_ref[...]
    for s in range(8):
        normed = (flat[pl.ds(s, 128, stride=8), :].T * out_gain).astype(BF16)
        proj = jnp.dot(normed, out_w_ref[...], preferred_element_type=F32)
        rows_out[pl.ds(s, 64, stride=16), :] = proj[:64]
        rows_out[pl.ds(8 + s, 64, stride=16), :] = proj[64:]
    out_ref[...] = (gate[...] * rows_out[...]).astype(BF16).reshape(64, 16, 128)
    pltpu.make_async_copy(osend.at[pl.ds(0, CHIPS - 1)], osend.at[pl.ds(0, CHIPS - 1)], osend_sem).wait()


def body(pair, pair_mask, norm_gain, left_weight, right_weight, gate_weight, out_gain, out_weight):
    vmem = pl.BlockSpec(memory_space=pltpu.VMEM)
    return pl.pallas_call(
        kernel,
        out_shape=jax.ShapeDtypeStruct((64, 16, 128), BF16),
        in_specs=[vmem] * 8,
        out_specs=vmem,
        scratch_shapes=[
            pltpu.VMEM((1024, 128), F32),
            pltpu.VMEM((2, 1024, 128), F32),
            pltpu.VMEM((2048, 128), F32),
            pltpu.VMEM((128, 16, 128), BF16),
            pltpu.VMEM((128, 16, 128), BF16),
            pltpu.VMEM((2, 256, 512), F32),
            pltpu.VMEM((256, 512), F32),
            pltpu.VMEM((128, 8, 128), BF16),
            pltpu.VMEM((128, 8, 128), BF16),
            pltpu.VMEM((1024, 128), F32),
            pltpu.VMEM((1024, 128), F32),
        ] + [pltpu.SemaphoreType.DMA(())] * 6,
        compiler_params=pltpu.CompilerParams(
            collective_id=0, has_side_effects=True, vmem_limit_bytes=40 * 1024 * 1024,
        ),
        name="triangle",
    )(
        pair, pair_mask, norm_gain.reshape(1, 128), left_weight, right_weight, gate_weight,
        out_gain.reshape(1, 128), out_weight,
    )


def solution(mesh):
    in_specs = (P("row", "col", None), P("row", "col"), P(), P(), P(), P(), P(), P())
    out_specs = P("row", "col", None)
    return jax.shard_map(body, mesh=mesh, in_specs=in_specs, out_specs=out_specs, check_vma=False)
```

time: 348 us -> 49.3 us (0.14)
  waiting for transfers between devices: 281 us -> 0 us
  Pallas kernels: 0 us -> 43.9 us
  local copies, waits for them, and re-layouts: 34.3 us -> 5 us
  between operations: 13.3 us -> 0.04 us
  matrix products: 8.8 us -> 0 us
  other arithmetic: 8.76 us -> 0 us
    all_gather x2 -> x0, waiting for transfers between devices: 175 us -> none  [the longest x1 91 us: body(): slab = lax.all_gather(right, 'col', axis=1, tiled=True)]
    psum x1 -> x0, waiting for transfers between devices: 105 us -> none  [from_root(): return lax.psum(jnp.where(mine, shard, jnp.zeros_like(shard)), axis)]
    pallas_call x0 -> x1, Pallas kernels: none -> 43.9 us  [body(): pl.pallas_call(kernel, out_shape=jax.ShapeDtypeStruct((64, 16, 128), BF16...]
    all_gather x1 -> x0, local copies, waits for them, and re-layouts: 29.2 us -> none  [body(): lax.all_gather(left, 'col', axis=1, tiled=True)]
    dot_general x5 -> x0, matrix products: 8.8 us -> none  [the longest x1 7.06 us: body(): jnp.einsum('ikh,jkh->ijh', lax.all_gather(left, 'col', axis=1, tiled=True...]
    unnamed x12 -> x16, local copies, waits for them, and re-layouts: 0.76 us -> 5 us
  transfers between devices with their start and end apart: 3 -> 0, of which waited for: 3 -> 0; matrix products, arithmetic and copies ran while one was open for 9% -> 0% of each run, Pallas kernels for 0% -> 0%
where the time goes in v1:
time: 49.3 us; the launch traced here: 49 us
  Pallas kernels  43.9 us (89%)
  local copies, waits for them, and re-layouts  5 us (10%)
    pallas_call x1, Pallas kernels, body(): pl.pallas_call(kernel, out_shape=jax.ShapeDtypeStruct((64, 16, 128), BF16...  43.9 us
    unnamed x16, local copies, waits for them, and re-layouts  5 us

profile of v1, /device:TPU:1, one launch (start us, length us, event | category | flops | bytes accessed | tf_op | source)
XLA Modules:
  0.0 49.0 jit_solution(18260812082801685023)
XLA Ops:
  0.0 0.0 copy-start.3
  0.0 0.0 copy-start.5
  0.0 0.0 copy-start.6
  0.0 0.8 %copy.9.mask_ref = s32[64,16]{1,0:T(8,128)S(1)} copy(s32[64,16]{0,1:T(8,128)} %param.9) | data formatting | bytes 8192 | tf_op args[1]
  0.8 0.0 copy-done.3
  0.8 0.0 copy-done.5
  0.8 0.0 copy-done.6
  0.8 0.0 copy-start
  0.9 1.0 %copy-done = f32[64,16,128]{2,1,0:T(8,128)S(1)} copy-done((f32[64,16,128]{2,1,0:T(8,128)S(1)}, f32[64,16,128]{2,1,0:T(8,128)}, u32[]{:S(2)}) %copy-start) | copy-done | bytes 524312
  1.9 0.0 copy-start.1
  1.9 0.8 %copy-done.1 = bf16[128,256]{1,0:T(8,128)(2,1)S(1)} copy-done((bf16[128,256]{1,0:T(8,128)(2,1)S(1)}, bf16[128,256]{1,0:T(8,128)(2,1)}, u32[]{:S(2)}) %copy-start.1) | copy-done | bytes 65560
  2.7 0.0 copy-start.2
  2.7 0.8 %copy-done.2 = bf16[128,256]{1,0:T(8,128)(2,1)S(1)} copy-done((bf16[128,256]{1,0:T(8,128)(2,1)S(1)}, bf16[128,256]{1,0:T(8,128)(2,1)}, u32[]{:S(2)}) %copy-start.2) | copy-done | bytes 65560
  3.6 0.0 copy-start.4
  3.6 0.8 %copy-done.4 = bf16[128,128]{1,0:T(8,128)(2,1)S(1)} copy-done((bf16[128,128]{1,0:T(8,128)(2,1)S(1)}, bf16[128,128]{1,0:T(8,128)(2,1)}, u32[]{:S(2)}) %copy-start.4) | copy-done | bytes 32792
  4.3 43.9 %triangle.1 = bf16[64,16,128]{2,1,0:T(8,128)(2,1)S(1)} custom-call(f32[64,16,128]{2,1,0:T(8,128)S(1)} %copy-done, s32[64,16]{1,0:T(8,128)S(1)} %copy.9.mask_ref, f32[1,128]{1,0:T(1,128)S(1)} %bitcast.2, bf16[128,256]{1,0:T(8,128)(2,1)S(1)} %copy-done.1, bf16[128,256]{1,0:T(8,128)(2,1)S(1)} %copy-done.2, bf16[128,128]{1,0:T(8,128)(2,1)S(1)} %copy-done.3, ...), custom_call_target="tpu_custom_call" | custom-call | tf_op jit(solution)/shard_map/triangle/pallas_call | solution.py:163
  48.3 0.7 %copy.11 = bf16[64,16,128]{2,1,0:T(8,128)(2,1)} copy(bf16[64,16,128]{2,1,0:T(8,128)(2,1)S(1)} %triangle.1) | data formatting | bytes 524288
Async XLA Ops:
  0.0 0.8 %copy-start.3 = (bf16[128,128]{1,0:T(8,128)(2,1)S(1)}, bf16[128,128]{1,0:T(8,128)(2,1)}, u32[]{:S(2)}) copy-start(bf16[128,128]{1,0:T(8,128)(2,1)} %gate_w_ref.1) | copy-start | bytes 98308
  0.0 0.8 %copy-start.5 = (f32[128]{0:T(128)S(1)}, f32[128]{0:T(128)}, u32[]{:S(2)}) copy-start(f32[128]{0:T(128)} %param.10) | copy-start | bytes 1540
  0.0 0.8 %copy-start.6 = (f32[128]{0:T(128)S(1)}, f32[128]{0:T(128)}, u32[]{:S(2)}) copy-start(f32[128]{0:T(128)} %param.14) | copy-start | bytes 1540
  0.8 1.0 %copy-start = (f32[64,16,128]{2,1,0:T(8,128)S(1)}, f32[64,16,128]{2,1,0:T(8,128)}, u32[]{:S(2)}) copy-start(f32[64,16,128]{2,1,0:T(8,128)} %pair_ref.1) | copy-start | bytes 1572868
  1.9 0.8 %copy-start.1 = (bf16[128,256]{1,0:T(8,128)(2,1)S(1)}, bf16[128,256]{1,0:T(8,128)(2,1)}, u32[]{:S(2)}) copy-start(bf16[128,256]{1,0:T(8,128)(2,1)} %left_w_ref.1) | copy-start | bytes 196612
  2.7 0.8 %copy-start.2 = (bf16[128,256]{1,0:T(8,128)(2,1)S(1)}, bf16[128,256]{1,0:T(8,128)(2,1)}, u32[]{:S(2)}) copy-start(bf16[128,256]{1,0:T(8,128)(2,1)} %right_w_ref.1) | copy-start | bytes 196612
  3.6 0.8 %copy-start.4 = (bf16[128,128]{1,0:T(8,128)(2,1)S(1)}, bf16[128,128]{1,0:T(8,128)(2,1)}, u32[]{:S(2)}) copy-start(bf16[128,128]{1,0:T(8,128)(2,1)} %out_w_ref.1) | copy-start | bytes 98308

commit v2 on v1

v2 whole, which is shorter than its diff:
```python
import jax
import jax.numpy as jnp
from jax import lax
from jax.experimental import pallas as pl
from jax.experimental.pallas import tpu as pltpu
from jax.sharding import PartitionSpec as P

F32 = jnp.float32
BF16 = jnp.bfloat16
EPS = 1e-05
CHIPS = 128


def hops(offset):
    dz, dy, dx = offset
    return min(dz, 8 - dz) + min(dy, 4 - dy) + min(dx, 4 - dx)


OFFSETS = sorted(
    ((dz, dy, dx) for dx in range(4) for dy in range(4) for dz in range(8) if dz or dy or dx),
    key=lambda offset: -hops(offset),
)
CHUNKS = (2, 0, 1, 3)


def rem(a, b):
    return lax.rem(a, jnp.int32(b))


def div(a, b):
    return lax.div(a, jnp.int32(b))


def kernel(
    pair_hbm, mask_hbm, norm_gain_hbm, left_w_hbm, right_w_hbm, gate_w_hbm, out_gain_hbm, out_w_hbm,
    out_ref,
    pair_ref, mask_ref, norm_gain_ref, left_w_ref, right_w_ref, gate_w_ref, out_gain_ref, out_w_ref, load_sem,
    gate, edges, packed, send, recv, left, right, part, other, osend, orecv, flat, rows_out,
    send_sem, recv_sem, osend_sem, orecv_sem, xsend_sem, xrecv_sem,
):
    row = lax.axis_index("row")
    col = lax.axis_index("col")
    core = rem(col, 2)
    x = rem(row, 4)
    y = rem(div(col, 2), 4)
    z = div(row, 4) * 4 + div(col, 8)
    me = row * 16 + div(col, 2)

    z_at = [rem(z + d, 8) for d in range(8)]
    y_at = [rem(y + d, 4) for d in range(4)]
    x_at = [rem(x + d, 4) for d in range(4)]

    def peer(offset):
        dz, dy, dx = offset
        prow = div(z_at[dz], 4) * 4 + x_at[dx]
        pchip = rem(z_at[dz], 4) * 4 + y_at[dy]
        return prow * 16 + pchip, (prow, pchip * 2 + core)

    loads = [
        pltpu.make_async_copy(source, target, load_sem.at[at])
        for at, (source, target) in enumerate((
            (pair_hbm, pair_ref), (norm_gain_hbm, norm_gain_ref), (left_w_hbm, left_w_ref),
            (right_w_hbm, right_w_ref), (gate_w_hbm, gate_w_ref), (mask_hbm, mask_ref),
            (out_gain_hbm, out_gain_ref), (out_w_hbm, out_w_ref),
        ))
    ]
    for load in loads:
        load.start()

    partner = {"col": col + 1 - 2 * core}

    barrier = pltpu.get_barrier_semaphore()

    for offset in OFFSETS:
        pl.semaphore_signal(barrier, inc=1, device_id=peer(offset)[1], device_id_type=pl.DeviceIdType.MESH)
    pl.semaphore_signal(barrier, inc=1, device_id=partner, device_id_type=pl.DeviceIdType.MESH)

    for load in loads:
        load.wait()
    gain = norm_gain_ref[...]
    for block in range(4):
        values = pair_ref[pl.ds(block * 16, 16)].reshape(256, 128)
        mean = jnp.mean(values, axis=-1, keepdims=True)
        centered = values - mean
        spread = jnp.mean(centered * centered, axis=-1, keepdims=True)
        normed = (centered * lax.rsqrt(spread + EPS) * gain).astype(BF16)
        here = pl.ds(block * 256, 256)
        for side, weight in ((0, left_w_ref), (1, right_w_ref)):
            proj = jnp.dot(normed, weight[...], preferred_element_type=F32)
            edges[side, here, :] = jax.nn.sigmoid(proj[:, :128]) * proj[:, 128:]
        gate[here, :] = jax.nn.sigmoid(jnp.dot(normed, gate_w_ref[...], preferred_element_type=F32))

    odd = rem(row, 2)
    for k in range(16):
        first = edges[odd, pl.ds(k, 64, stride=16), :]
        second = edges[1 - odd, pl.ds(k, 64, stride=16), :]
        packed[pl.ds(k, 128, stride=16), :] = jnp.concatenate([first, second], axis=0).T
    mask = mask_ref[...].astype(F32)
    mask = jnp.concatenate([mask, mask], axis=1)
    send[...] = (packed[...].reshape(128, 16, 128) * mask[None]).astype(BF16)

    pl.semaphore_wait(barrier, CHIPS)

    own = pltpu.make_async_copy(send.at[me], recv.at[me], recv_sem)
    own.start()

    for offset in OFFSETS:
        there, device = peer(offset)
        pltpu.make_async_remote_copy(
            src_ref=send.at[there], dst_ref=recv.at[me], send_sem=send_sem, recv_sem=recv_sem,
            device_id=device, device_id_type=pl.DeviceIdType.MESH,
        ).start()
    pltpu.make_async_copy(recv, recv, recv_sem).wait()

    low = lax.broadcasted_iota(jnp.int32, (256, 128), 1) < 64
    for pair_at in range(4):
        even = recv[pl.ds(pair_at * 32, 16)].reshape(256, 128)
        uneven = recv[pl.ds(pair_at * 32 + 16, 16)].reshape(256, 128)
        here = pl.ds(pair_at * 256, 256)
        left[:, pair_at * 128:(pair_at + 1) * 128] = jnp.where(low, even, uneven)
        right[here, :] = jnp.where(low, uneven, even)

    swaps = []
    for at, dz in enumerate(CHUNKS):
        zone = rem(z_at[dz], 4)
        products = lax.dot_general(
            right[pl.ds(pl.multiple_of(zone * 256, 256), 256), :], left[...], (((0,), (0,)), ((), ())),
            preferred_element_type=F32,
        )
        for half in range(2):
            for q in range(4):
                source = half * 64 + q * 16
                part[at, q % 2, pl.ds((1 - half) * 32 + q // 2 * 16, 16), :] = products[source:source + 16]
        swap = pltpu.make_async_remote_copy(
            src_ref=part.at[at, 1 - core], dst_ref=other.at[at], send_sem=xsend_sem.at[at], recv_sem=xrecv_sem.at[at],
            device_id=partner, device_id_type=pl.DeviceIdType.MESH,
        )
        swap.start()
        swaps.append(swap)

    low8 = lax.broadcasted_iota(jnp.int32, (32, 128), 1) < 64
    own_back = pltpu.make_async_copy(osend.at[me], orecv.at[me], orecv_sem)
    for at, dz in enumerate(CHUNKS):
        swaps[at].wait_recv()
        zone = rem(z_at[dz], 4)
        for pair_at in range(4):
            lanes = pl.ds(pair_at * 128, 128)
            total = (part[at, core, :, lanes] + other[at, :, lanes]).reshape(4, 2, 8, 128)
            top = total[:, 0].reshape(32, 128)
            bottom = total[:, 1].reshape(32, 128)
            even = jnp.where(low8, top, pltpu.roll(bottom, 64, 1))
            uneven = jnp.where(low8, pltpu.roll(top, 64, 1), bottom)
            osend[pl.ds(pair_at * 32 + zone * 4, 4)] = even.reshape(4, 8, 128).astype(BF16)
            osend[pl.ds(pair_at * 32 + 16 + zone * 4, 4)] = uneven.reshape(4, 8, 128).astype(BF16)
        if dz == 0:
            own_back.start()
        for offset in OFFSETS:
            if offset[0] % 4 == dz:
                there, device = peer(offset)
                pltpu.make_async_remote_copy(
                    src_ref=osend.at[there], dst_ref=orecv.at[me], send_sem=osend_sem, recv_sem=orecv_sem,
                    device_id=device, device_id_type=pl.DeviceIdType.MESH,
                ).start()
    for swap in swaps:
        swap.wait_send()
    pltpu.make_async_copy(send.at[pl.ds(0, CHIPS - 1)], send.at[pl.ds(0, CHIPS - 1)], send_sem).wait()
    pltpu.make_async_copy(orecv, orecv, orecv_sem).wait()

    tri = orecv[...].astype(F32)
    mean = jnp.sum(tri, axis=0, keepdims=True) * (1.0 / 128)
    centered = tri - mean
    spread = jnp.sum(centered * centered, axis=0, keepdims=True) * (1.0 / 128)
    flat[...] = (centered * lax.rsqrt(spread + EPS)).reshape(1024, 128)
    out_gain = out_gain_ref[...]
    for s in range(8):
        normed = (flat[pl.ds(s, 128, stride=8), :].T * out_gain).astype(BF16)
        proj = jnp.dot(normed, out_w_ref[...], preferred_element_type=F32)
        rows_out[pl.ds(s, 64, stride=16), :] = proj[:64]
        rows_out[pl.ds(8 + s, 64, stride=16), :] = proj[64:]
    out_ref[...] = (gate[...] * rows_out[...]).astype(BF16).reshape(64, 16, 128)
    pltpu.make_async_copy(osend.at[pl.ds(0, CHIPS - 1)], osend.at[pl.ds(0, CHIPS - 1)], osend_sem).wait()


def body(pair, pair_mask, norm_gain, left_weight, right_weight, gate_weight, out_gain, out_weight):
    vmem = pl.BlockSpec(memory_space=pltpu.VMEM)
    return pl.pallas_call(
        kernel,
        out_shape=jax.ShapeDtypeStruct((64, 16, 128), BF16),
        in_specs=[pl.BlockSpec(memory_space=pltpu.HBM)] * 8,
        out_specs=vmem,
        scratch_shapes=[
            pltpu.VMEM((64, 16, 128), F32),
            pltpu.VMEM((16, 64), jnp.int32),
            pltpu.VMEM((1, 128), F32),
            pltpu.VMEM((128, 256), BF16),
            pltpu.VMEM((128, 256), BF16),
            pltpu.VMEM((128, 128), BF16),
            pltpu.VMEM((1, 128), F32),
            pltpu.VMEM((128, 128), BF16),
            pltpu.SemaphoreType.DMA((8,)),
            pltpu.VMEM((1024, 128), F32),
            pltpu.VMEM((2, 1024, 128), F32),
            pltpu.VMEM((2048, 128), F32),
            pltpu.VMEM((128, 16, 128), BF16),
            pltpu.VMEM((128, 16, 128), BF16),
            pltpu.VMEM((256, 512), BF16),
            pltpu.VMEM((1024, 128), BF16),
            pltpu.VMEM((4, 2, 64, 512), F32),
            pltpu.VMEM((4, 64, 512), F32),
            pltpu.VMEM((128, 8, 128), BF16),
            pltpu.VMEM((128, 8, 128), BF16),
            pltpu.VMEM((1024, 128), F32),
            pltpu.VMEM((1024, 128), F32),
        ] + [pltpu.SemaphoreType.DMA(())] * 4 + [pltpu.SemaphoreType.DMA((4,))] * 2,
        compiler_params=pltpu.CompilerParams(
            collective_id=0, has_side_effects=True, vmem_limit_bytes=56 * 1024 * 1024,
        ),
        name="triangle",
    )(
        pair, pair_mask.T, norm_gain.reshape(1, 128), left_weight, right_weight, gate_weight,
        out_gain.reshape(1, 128), out_weight,
    )


def solution(mesh):
    in_specs = (P("row", "col", None), P("row", "col"), P(), P(), P(), P(), P(), P())
    out_specs = P("row", "col", None)
    return jax.shard_map(body, mesh=mesh, in_specs=in_specs, out_specs=out_specs, check_vma=False)
```

time: 49.3 us -> 42.1 us (0.85)
  Pallas kernels: 43.9 us -> 40.4 us
  local copies, waits for them, and re-layouts: 5 us -> 1.67 us
    pallas_call x1, Pallas kernels: 43.9 us -> 40.4 us  [body(): pl.pallas_call(kernel, out_shape=jax.ShapeDtypeStruct((64, 16, 128), BF16...]
    unnamed x16 -> x1, local copies, waits for them, and re-layouts: 5 us -> 1.67 us
where the time goes in v2:
time: 42.1 us; the launch traced here: 42 us
  Pallas kernels  40.4 us (96%)
  local copies, waits for them, and re-layouts  1.67 us (4%)
    pallas_call x1, Pallas kernels, body(): pl.pallas_call(kernel, out_shape=jax.ShapeDtypeStruct((64, 16, 128), BF16...  40.4 us
    unnamed x1, local copies, waits for them, and re-layouts  1.67 us

profile of v2, /device:TPU:1, one launch (start us, length us, event | category | flops | bytes accessed | tf_op | source)
XLA Modules:
  0.0 42.0 jit_solution(15246891757242875954)
XLA Ops:
  0.0 40.4 %triangle.1 = bf16[64,16,128]{2,1,0:T(8,128)(2,1)} custom-call(f32[64,16,128]{2,1,0:T(8,128)} %pair_hbm.1, s32[16,64]{1,0:T(8,128)} %bitcast.3, f32[1,128]{1,0:T(1,128)} %bitcast.4, bf16[128,256]{1,0:T(8,128)(2,1)} %left_w_hbm.1, bf16[128,256]{1,0:T(8,128)(2,1)} %right_w_hbm.1, bf16[128,128]{1,0:T(8,128)(2,1)} %gate_w_hbm.1, f32[1,128]{1,0:T(1,128)} %bitcast.5, ...), custom_call_target="tpu_custom_call" | custom-call | tf_op jit(solution)/shard_map/triangle/pallas_call | solution.py:186
  40.4 1.7 %copy.10 = bf16[64,16,128]{2,1,0:T(8,128)(2,1)} copy(bf16[64,16,128]{2,1,0:T(8,128)(2,1)} %triangle.1) | data formatting | bytes 524288

commit v3 on v2

v3 whole, which is shorter than its diff:
```python
import jax
import jax.numpy as jnp
from jax import lax
from jax.experimental import pallas as pl
from jax.experimental.pallas import tpu as pltpu
from jax.sharding import PartitionSpec as P

F32 = jnp.float32
BF16 = jnp.bfloat16
EPS = 1e-05
CHIPS = 128


def hops(offset):
    dz, dy, dx = offset
    return min(dz, 8 - dz) + min(dy, 4 - dy) + min(dx, 4 - dx)


OFFSETS = sorted(
    ((dz, dy, dx) for dx in range(4) for dy in range(4) for dz in range(8) if dz or dy or dx),
    key=lambda offset: -hops(offset),
)
GREETED = sorted(
    ((dz, dy, dx, dc) for dc in range(2) for dx in range(2) for dy in range(4) for dz in range(8)),
    key=lambda offset: -hops((offset[0], offset[1], 2 * offset[2])),
)
BITS = [(zh, xs, yu, zt, dc) for zh in (1, 0) for xs in (1, 0) for yu in (1, 0) for zt in (1, 0) for dc in (0, 1)]
MESH = pl.DeviceIdType.MESH


def rem(a, b):
    return lax.rem(a, jnp.int32(b))


def div(a, b):
    return lax.div(a, jnp.int32(b))


def kernel(
    pair_hbm, mask_hbm, norm_gain_hbm, left_w_hbm, right_w_hbm, gate_w_hbm, out_gain_hbm, out_w_hbm,
    out_ref,
    pair_ref, mask_ref, norm_gain_ref, left_w_ref, right_w_ref, gate_w_ref, out_gain_ref, out_w_ref, load_sem,
    gate, edges, packed, send, recv, left, right, osend, orecv, flat, rows_out,
    send_sem, recv_sem, osend_sem, orecv_sem, xsend_sem, xrecv_sem,
):
    row = lax.axis_index("row")
    col = lax.axis_index("col")
    core = rem(col, 2)
    x = rem(row, 4)
    y = rem(div(col, 2), 4)
    z = div(row, 4) * 4 + div(col, 8)
    me = row * 16 + div(col, 2)

    z_at = [rem(z + d, 8) for d in range(8)]
    y_at = [rem(y + d, 4) for d in range(4)]
    x_at = [rem(x + d, 4) for d in range(4)]

    def peer(offset):
        dz, dy, dx = offset
        prow = div(z_at[dz], 4) * 4 + x_at[dx]
        pchip = rem(z_at[dz], 4) * 4 + y_at[dy]
        return prow * 16 + pchip, (prow, pchip * 2 + side)

    side = rem(x, 2)
    home = rem(x + core, 2)
    slot = (div(z, 4) * 2 + div(x, 2)) * 32 + col
    x_half = [rem(div(x, 2) + d, 2) for d in range(2)]
    core_at = [rem(core + d, 2) for d in range(2)]

    loads = [
        pltpu.make_async_copy(source, target, load_sem.at[at])
        for at, (source, target) in enumerate((
            (pair_hbm, pair_ref), (norm_gain_hbm, norm_gain_ref), (left_w_hbm, left_w_ref),
            (right_w_hbm, right_w_ref), (gate_w_hbm, gate_w_ref), (mask_hbm, mask_ref),
            (out_gain_hbm, out_gain_ref), (out_w_hbm, out_w_ref),
        ))
    ]
    for load in loads:
        load.start()

    partner = {"col": col + 1 - 2 * core}

    barrier = pltpu.get_barrier_semaphore()

    def greet(offset):
        dz, dy, dx, dc = offset
        device = (div(z_at[dz], 4) * 4 + core + 2 * x_half[dx], rem(z_at[dz], 4) * 8 + y_at[dy] * 2 + core_at[dc])
        pl.semaphore_signal(barrier, inc=1, device_id=device, device_id_type=MESH)

    for offset in GREETED:
        if offset[:3] != (0, 0, 0):
            greet(offset)
    pl.semaphore_signal(barrier, inc=1, device_id=partner, device_id_type=MESH)

    @pl.when(home != 0)
    def _():
        greet((0, 0, 0, 0))
        greet((0, 0, 0, 1))

    for load in loads:
        load.wait()
    gain = norm_gain_ref[...]
    for block in range(4):
        values = pair_ref[pl.ds(block * 16, 16)].reshape(256, 128)
        mean = jnp.mean(values, axis=-1, keepdims=True)
        centered = values - mean
        spread = jnp.mean(centered * centered, axis=-1, keepdims=True)
        normed = (centered * lax.rsqrt(spread + EPS) * gain).astype(BF16)
        here = pl.ds(block * 256, 256)
        for which, weight in ((0, left_w_ref), (1, right_w_ref)):
            proj = jnp.dot(normed, weight[...], preferred_element_type=F32)
            edges[which, here, :] = jax.nn.sigmoid(proj[:, :128]) * proj[:, 128:]
        gate[here, :] = jax.nn.sigmoid(jnp.dot(normed, gate_w_ref[...], preferred_element_type=F32))

    odd = div(x, 2)
    for k in range(16):
        first = edges[odd, pl.ds(k, 64, stride=16), :]
        second = edges[1 - odd, pl.ds(k, 64, stride=16), :]
        packed[pl.ds(k, 128, stride=16), :] = jnp.concatenate([first, second], axis=0).T
    mask = mask_ref[...].astype(F32)
    mask = jnp.concatenate([mask, mask], axis=1)
    send[...] = (packed[...].reshape(128, 16, 128) * mask[None]).astype(BF16)

    pl.semaphore_wait(barrier, CHIPS)

    @pl.when(home == 0)
    def _():
        pltpu.make_async_copy(send.at[me], recv.at[slot], recv_sem).start()

    @pl.when(home != 0)
    def _():
        pltpu.make_async_remote_copy(
            src_ref=send.at[me], dst_ref=recv.at[slot], send_sem=send_sem, recv_sem=recv_sem,
            device_id=partner, device_id_type=MESH,
        ).start()

    for offset in OFFSETS:
        there, device = peer(offset)
        pltpu.make_async_remote_copy(
            src_ref=send.at[there], dst_ref=recv.at[slot], send_sem=send_sem, recv_sem=recv_sem,
            device_id=device, device_id_type=MESH,
        ).start()
    pltpu.make_async_copy(recv, recv, recv_sem).wait()

    low = lax.broadcasted_iota(jnp.int32, (512, 128), 1) < 64
    swaps = []
    for zh in range(2):
        first = recv[pl.ds(zh * 64, 32)].reshape(512, 128)
        second = recv[pl.ds(zh * 64 + 32, 32)].reshape(512, 128)
        left[:, zh * 128:(zh + 1) * 128] = jnp.where(low, first, second)
        right[0, zh] = jnp.where(low, second, first)
    for zh in range(2):
        swap = pltpu.make_async_remote_copy(
            src_ref=right.at[0, zh], dst_ref=right.at[1, zh], send_sem=xsend_sem.at[zh], recv_sem=xrecv_sem.at[zh],
            device_id=partner, device_id_type=MESH,
        )
        swap.start()
        swaps.append(swap)

    low8 = lax.broadcasted_iota(jnp.int32, (64, 128), 1) < 64
    for whose in range(2):
        if whose == 1:
            for swap in swaps:
                swap.wait_recv()
        x_low = core if whose == 0 else 1 - core
        for dp in (1, 0):
            zone = rem(div(rem(z, 4), 2) + dp, 2)
            products = lax.dot_general(
                right[whose, zone], left[...], (((0,), (0,)), ((), ())), preferred_element_type=F32
            )
            for zh in range(2):
                block = products[:, zh * 128:(zh + 1) * 128].reshape(8, 2, 8, 128)
                top = block[:, 0].reshape(64, 128)
                bottom = block[:, 1].reshape(64, 128)
                even = jnp.where(low8, top, pltpu.roll(bottom, 64, 1)).reshape(8, 8, 128).astype(BF16)
                uneven = jnp.where(low8, pltpu.roll(top, 64, 1), bottom).reshape(8, 8, 128).astype(BF16)
                for xs, values in ((0, even), (1, uneven)):
                    for half in range(2):
                        at = (zh * 2 + xs) * 32 + zone * 16 + (1 - half) * 8 + x_low * 4
                        osend[pl.ds(at, 4)] = values[half * 4:half * 4 + 4]

            def give_back(bits):
                zh, xs, yu, zt, dc = bits
                pz = rem(div(z, 4) + zh, 2)
                prow = pz * 4 + core + 2 * x_half[xs]
                pcol = (zone * 2 + rem(z + zt, 2)) * 8 + (2 * x_low + rem(y + yu, 2)) * 2 + core_at[dc]
                return (pz * 2 + x_half[xs]) * 32 + pcol, (prow, pcol)

            def send_back(bits):
                there, device = give_back(bits)
                pltpu.make_async_remote_copy(
                    src_ref=osend.at[there], dst_ref=orecv.at[me], send_sem=osend_sem, recv_sem=orecv_sem,
                    device_id=device, device_id_type=MESH,
                ).start()

            for bits in BITS:
                if dp == 0 and bits == (0, 0, 0, 0, 0):
                    mine = home + lax.abs(div(y, 2) - x_low) == 0

                    @pl.when(mine)
                    def _():
                        pltpu.make_async_copy(osend.at[slot], orecv.at[me], orecv_sem).start()

                    @pl.when(jnp.logical_not(mine))
                    def _():
                        send_back(bits)
                else:
                    send_back(bits)
    for swap in swaps:
        swap.wait_send()
    pltpu.make_async_copy(send.at[pl.ds(0, CHIPS - 1)], send.at[pl.ds(0, CHIPS - 1)], send_sem).wait()

    @pl.when(home != 0)
    def _():
        pltpu.make_async_copy(send.at[0], send.at[0], send_sem).wait()
    pltpu.make_async_copy(orecv, orecv, orecv_sem).wait()

    tri = orecv[...].astype(F32)
    mean = jnp.sum(tri, axis=0, keepdims=True) * (1.0 / 128)
    centered = tri - mean
    spread = jnp.sum(centered * centered, axis=0, keepdims=True) * (1.0 / 128)
    flat[...] = (centered * lax.rsqrt(spread + EPS)).reshape(1024, 128)
    out_gain = out_gain_ref[...]
    for s in range(8):
        normed = (flat[pl.ds(s, 128, stride=8), :].T * out_gain).astype(BF16)
        proj = jnp.dot(normed, out_w_ref[...], preferred_element_type=F32)
        rows_out[pl.ds(s, 64, stride=16), :] = proj[:64]
        rows_out[pl.ds(8 + s, 64, stride=16), :] = proj[64:]
    out_ref[...] = (gate[...] * rows_out[...]).astype(BF16).reshape(64, 16, 128)
    pltpu.make_async_copy(osend.at[pl.ds(0, CHIPS - 1)], osend.at[pl.ds(0, CHIPS - 1)], osend_sem).wait()

    @pl.when(home != 0)
    def _():
        pltpu.make_async_copy(osend.at[0], osend.at[0], osend_sem).wait()


def body(pair, pair_mask, norm_gain, left_weight, right_weight, gate_weight, out_gain, out_weight):
    vmem = pl.BlockSpec(memory_space=pltpu.VMEM)
    return pl.pallas_call(
        kernel,
        out_shape=pltpu.VMEM((64, 16, 128), BF16),
        in_specs=[pl.BlockSpec(memory_space=pltpu.HBM)] * 8,
        out_specs=vmem,
        scratch_shapes=[
            pltpu.VMEM((64, 16, 128), F32),
            pltpu.VMEM((16, 64), jnp.int32),
            pltpu.VMEM((1, 128), F32),
            pltpu.VMEM((128, 256), BF16),
            pltpu.VMEM((128, 256), BF16),
            pltpu.VMEM((128, 128), BF16),
            pltpu.VMEM((1, 128), F32),
            pltpu.VMEM((128, 128), BF16),
            pltpu.SemaphoreType.DMA((8,)),
            pltpu.VMEM((1024, 128), F32),
            pltpu.VMEM((2, 1024, 128), F32),
            pltpu.VMEM((2048, 128), F32),
            pltpu.VMEM((128, 16, 128), BF16),
            pltpu.VMEM((128, 16, 128), BF16),
            pltpu.VMEM((512, 256), BF16),
            pltpu.VMEM((2, 2, 512, 128), BF16),
            pltpu.VMEM((128, 8, 128), BF16),
            pltpu.VMEM((128, 8, 128), BF16),
            pltpu.VMEM((1024, 128), F32),
            pltpu.VMEM((1024, 128), F32),
        ] + [pltpu.SemaphoreType.DMA(())] * 4 + [pltpu.SemaphoreType.DMA((2,))] * 2,
        compiler_params=pltpu.CompilerParams(
            collective_id=0, has_side_effects=True, vmem_limit_bytes=40 * 1024 * 1024,
        ),
        name="triangle",
    )(
        *(pltpu.with_memory_space_constraint(a, pltpu.HBM) for a in (pair, pair_mask.T, norm_gain.reshape(1, 128), left_weight, right_weight, gate_weight,
        out_gain.reshape(1, 128), out_weight))
    )


def solution(mesh):
    in_specs = (P("row", "col", None), P("row", "col"), P(), P(), P(), P(), P(), P())
    out_specs = P("row", "col", None)
    return jax.shard_map(body, mesh=mesh, in_specs=in_specs, out_specs=out_specs, check_vma=False)
```

time: 42.1 us -> 38.7 us (0.919); the launches traced: 42 us -> 38.2 us
  Pallas kernels: 40.4 us -> 37.5 us
  local copies, waits for them, and re-layouts: 1.67 us -> 0.71 us
    pallas_call x1, Pallas kernels: 40.4 us -> 37.5 us  [body(): pl.pallas_call(kernel, out_shape=pltpu.VMEM((64, 16, 128), BF16), in_spec...]
    unnamed x1, local copies, waits for them, and re-layouts: 1.67 us -> 0.71 us
where the time goes in v3:
time: 38.7 us; the launch traced here: 38.2 us
  Pallas kernels  37.5 us (97%)
  local copies, waits for them, and re-layouts  0.71 us (2%)
    pallas_call x1, Pallas kernels, body(): pl.pallas_call(kernel, out_shape=pltpu.VMEM((64, 16, 128), BF16), in_spec...  37.5 us

profile of v3, /device:TPU:1, one launch (start us, length us, event | category | flops | bytes accessed | tf_op | source)
XLA Modules:
  0.0 38.2 jit_solution(16400389611267729010)
XLA Ops:
  0.0 37.5 %triangle.1 = bf16[64,16,128]{2,1,0:T(8,128)(2,1)S(1)} custom-call(f32[64,16,128]{2,1,0:T(8,128)} %pair_hbm.1, s32[16,64]{1,0:T(8,128)} %bitcast.3, f32[1,128]{1,0:T(1,128)} %bitcast.4, bf16[128,256]{1,0:T(8,128)(2,1)} %left_w_hbm.1, bf16[128,256]{1,0:T(8,128)(2,1)} %right_w_hbm.1, bf16[128,128]{1,0:T(8,128)(2,1)} %gate_w_hbm.1, f32[1,128]{1,0:T(1,128)} %bitcast.5, ...), custom_call_target="tpu_custom_call" | custom-call | tf_op jit(solution)/shard_map/triangle/pallas_call | solution.py:239
  37.5 0.7 %copy.10 = bf16[64,16,128]{2,1,0:T(8,128)(2,1)} copy(bf16[64,16,128]{2,1,0:T(8,128)(2,1)S(1)} %triangle.1) | data formatting | bytes 524288

commit v4 on v2

v4 whole, which is shorter than its diff:
```python
import jax
import jax.numpy as jnp
from jax import lax
from jax.experimental import pallas as pl
from jax.experimental.pallas import tpu as pltpu
from jax.sharding import PartitionSpec as P

F32 = jnp.float32
BF16 = jnp.bfloat16
EPS = 1e-05
CHIPS = 128


def hops(offset):
    dz, dy, dx = offset
    return min(dz, 8 - dz) + min(dy, 4 - dy) + min(dx, 4 - dx)


OFFSETS = sorted(
    ((dz, dy, dx) for dx in range(4) for dy in range(4) for dz in range(8) if dz or dy or dx),
    key=lambda offset: -hops(offset),
)
MESH = pl.DeviceIdType.MESH


def rem(a, b):
    return lax.rem(a, jnp.int32(b))


def div(a, b):
    return lax.div(a, jnp.int32(b))


def kernel(
    pair_hbm, mask_hbm, norm_gain_hbm, left_w_hbm, right_w_hbm, gate_w_hbm, out_gain_hbm, out_w_hbm,
    out_ref,
    pair_ref, mask_ref, norm_gain_ref, left_w_ref, right_w_ref, gate_w_ref, out_gain_ref, out_w_ref, load_sem,
    gate, edges, packed, send_left, send_right, mixed, recv, recv_right, left, right, osend, orecv, flat, rows_out,
    send_sem, recv_sem, mix_send_sem, mix_recv_sem, swap_send_sem, swap_recv_sem, osend_sem, orecv_sem,
):
    row = lax.axis_index("row")
    col = lax.axis_index("col")
    core = rem(col, 2)
    x = rem(row, 4)
    y = rem(div(col, 2), 4)
    z = div(row, 4) * 4 + div(col, 8)
    me = row * 16 + div(col, 2)

    z_at = [rem(z + d, 8) for d in range(8)]
    y_at = [rem(y + d, 4) for d in range(4)]
    x_at = [rem(x + d, 4) for d in range(4)]

    def peer(offset):
        dz, dy, dx = offset
        prow = div(z_at[dz], 4) * 4 + x_at[dx]
        pchip = rem(z_at[dz], 4) * 4 + y_at[dy]
        return prow * 16 + pchip, (prow, pchip * 2 + core)

    loads = [
        pltpu.make_async_copy(source, target, load_sem.at[at])
        for at, (source, target) in enumerate((
            (pair_hbm, pair_ref), (norm_gain_hbm, norm_gain_ref), (left_w_hbm, left_w_ref),
            (right_w_hbm, right_w_ref), (gate_w_hbm, gate_w_ref), (mask_hbm, mask_ref),
            (out_gain_hbm, out_gain_ref), (out_w_hbm, out_w_ref),
        ))
    ]
    for load in loads:
        load.start()

    partner = {"col": col + 1 - 2 * core}

    barrier = pltpu.get_barrier_semaphore()

    for offset in OFFSETS:
        pl.semaphore_signal(barrier, inc=1, device_id=peer(offset)[1], device_id_type=MESH)
    pl.semaphore_signal(barrier, inc=1, device_id=partner, device_id_type=MESH)

    for load in loads:
        load.wait()
    gain = norm_gain_ref[...]
    for block in range(4):
        values = pair_ref[pl.ds(block * 16, 16)].reshape(256, 128)
        mean = jnp.mean(values, axis=-1, keepdims=True)
        centered = values - mean
        spread = jnp.mean(centered * centered, axis=-1, keepdims=True)
        normed = (centered * lax.rsqrt(spread + EPS) * gain).astype(BF16)
        here = pl.ds(block * 256, 256)
        for which, weight in ((0, left_w_ref), (1, right_w_ref)):
            proj = jnp.dot(normed, weight[...], preferred_element_type=F32)
            edges[which, here, :] = jax.nn.sigmoid(proj[:, :128]) * proj[:, 128:]
        gate[here, :] = jax.nn.sigmoid(jnp.dot(normed, gate_w_ref[...], preferred_element_type=F32))

    mask = mask_ref[...].astype(F32)
    left_mask = jnp.concatenate([mask[:8], mask[8:]], axis=1)
    right_lanes = [(high, q) for parity in range(2) for high in range(2) for q in (parity, parity + 2)]
    right_mask = jnp.concatenate([mask[high * 8:high * 8 + 8, q * 16:q * 16 + 16] for high, q in right_lanes], axis=1)
    for k in range(8):
        rows = [edges[0, pl.ds(high * 8 + k, 64, stride=16), :] for high in range(2)]
        packed[0, pl.ds(k, 128, stride=8), :] = jnp.concatenate(rows, axis=0).T
    send_left[...] = (packed[0].reshape(128, 8, 128) * left_mask[None]).astype(BF16)
    for k in range(8):
        rows = [edges[1, pl.ds(q * 256 + high * 8 + k, 16, stride=16), :] for high, q in right_lanes]
        packed[1, pl.ds(k, 128, stride=8), :] = jnp.concatenate(rows, axis=0).T
    mixed[0] = (packed[1].reshape(128, 8, 128) * right_mask[None]).astype(BF16)

    pl.semaphore_wait(barrier, CHIPS)

    def scatter(source, target, sem):
        pltpu.make_async_copy(source.at[me], target.at[me], sem).start()
        for offset in OFFSETS:
            there, device = peer(offset)
            pltpu.make_async_remote_copy(
                src_ref=source.at[there], dst_ref=target.at[me], send_sem=send_sem, recv_sem=sem,
                device_id=device, device_id_type=MESH,
            ).start()

    mix = pltpu.make_async_remote_copy(
        src_ref=mixed.at[0], dst_ref=mixed.at[1], send_sem=mix_send_sem, recv_sem=mix_recv_sem,
        device_id=partner, device_id_type=MESH,
    )
    mix.start()
    scatter(send_left, recv.at[0], recv_sem.at[0])
    mix.wait_recv()
    mine = lax.broadcasted_iota(jnp.int32, (1024, 128), 1) // 64 == core
    theirs = pltpu.roll(mixed[1].astype(F32).reshape(1024, 128), 64, 1)
    send_right[...] = jnp.where(mine, mixed[0].astype(F32).reshape(1024, 128), theirs).reshape(128, 8, 128).astype(BF16)
    scatter(send_right, recv_right, recv_sem.at[1])

    pltpu.make_async_copy(recv.at[0], recv.at[0], recv_sem.at[0]).wait()
    swap = pltpu.make_async_remote_copy(
        src_ref=recv.at[0], dst_ref=recv.at[1], send_sem=swap_send_sem, recv_sem=swap_recv_sem,
        device_id=partner, device_id_type=MESH,
    )
    swap.start()
    low = lax.broadcasted_iota(jnp.int32, (128, 128), 1) < 64
    for whose in range(2):
        if whose == 1:
            swap.wait_recv()
        tokens = pl.multiple_of((core if whose == 0 else 1 - core) * 256, 256)
        for pair_at in range(4):
            first = recv[whose, pl.ds(pair_at * 32, 16)].astype(F32).reshape(128, 128)
            second = recv[whose, pl.ds(pair_at * 32 + 16, 16)].astype(F32).reshape(128, 128)
            lanes = pl.ds(pair_at * 128, 128)
            left[pl.ds(tokens, 128), lanes] = jnp.where(low, first, pltpu.roll(second, 64, 1)).astype(BF16)
            left[pl.ds(tokens + 128, 128), lanes] = jnp.where(low, pltpu.roll(first, 64, 1), second).astype(BF16)

    pltpu.make_async_copy(recv_right, recv_right, recv_sem.at[1]).wait()
    for r in range(8):
        turned = recv_right[pl.ds(r * 16, 16)].astype(F32).reshape(128, 128).astype(BF16).T
        for group in range(4):
            right[pl.ds(r * 32, 32), pl.ds(group * 128, 128)] = turned[group * 32:group * 32 + 32]

    low8 = lax.broadcasted_iota(jnp.int32, (128, 128), 1) < 64
    for quarter in range(4):
        products = jnp.dot(
            right[...], left[:, quarter * 128:(quarter + 1) * 128], preferred_element_type=F32
        ).reshape(16, 2, 8, 128)
        top = products[:, 0].reshape(128, 128)
        bottom = products[:, 1].reshape(128, 128)
        even = jnp.where(low8, top, pltpu.roll(bottom, 64, 1))
        uneven = jnp.where(low8, pltpu.roll(top, 64, 1), bottom)
        osend[pl.ds(quarter * 32, 16)] = even.reshape(16, 8, 128).astype(BF16)
        osend[pl.ds(quarter * 32 + 16, 16)] = uneven.reshape(16, 8, 128).astype(BF16)

    pltpu.make_async_copy(osend.at[me], orecv.at[me], orecv_sem).start()
    for offset in OFFSETS:
        there, device = peer(offset)
        pltpu.make_async_remote_copy(
            src_ref=osend.at[there], dst_ref=orecv.at[me], send_sem=osend_sem, recv_sem=orecv_sem,
            device_id=device, device_id_type=MESH,
        ).start()

    mix.wait_send()
    swap.wait_send()
    for source in (send_left, send_right):
        pltpu.make_async_copy(source.at[pl.ds(0, CHIPS - 1)], source.at[pl.ds(0, CHIPS - 1)], send_sem).wait()
    pltpu.make_async_copy(orecv, orecv, orecv_sem).wait()

    tri = orecv[...].astype(F32)
    mean = jnp.sum(tri, axis=0, keepdims=True) * (1.0 / 128)
    centered = tri - mean
    spread = jnp.sum(centered * centered, axis=0, keepdims=True) * (1.0 / 128)
    flat[...] = (centered * lax.rsqrt(spread + EPS)).reshape(1024, 128)
    out_gain = out_gain_ref[...]
    for s in range(8):
        normed = (flat[pl.ds(s, 128, stride=8), :].T * out_gain).astype(BF16)
        proj = jnp.dot(normed, out_w_ref[...], preferred_element_type=F32)
        rows_out[pl.ds(s, 64, stride=16), :] = proj[:64]
        rows_out[pl.ds(8 + s, 64, stride=16), :] = proj[64:]
    out_ref[...] = (gate[...] * rows_out[...]).astype(BF16).reshape(64, 16, 128)
    pltpu.make_async_copy(osend.at[pl.ds(0, CHIPS - 1)], osend.at[pl.ds(0, CHIPS - 1)], osend_sem).wait()


def body(pair, pair_mask, norm_gain, left_weight, right_weight, gate_weight, out_gain, out_weight):
    vmem = pl.BlockSpec(memory_space=pltpu.VMEM)
    return pl.pallas_call(
        kernel,
        out_shape=pltpu.VMEM((64, 16, 128), BF16),
        in_specs=[pl.BlockSpec(memory_space=pltpu.HBM)] * 8,
        out_specs=vmem,
        scratch_shapes=[
            pltpu.VMEM((64, 16, 128), F32),
            pltpu.VMEM((16, 64), jnp.int32),
            pltpu.VMEM((1, 128), F32),
            pltpu.VMEM((128, 256), BF16),
            pltpu.VMEM((128, 256), BF16),
            pltpu.VMEM((128, 128), BF16),
            pltpu.VMEM((1, 128), F32),
            pltpu.VMEM((128, 128), BF16),
            pltpu.SemaphoreType.DMA((8,)),
            pltpu.VMEM((1024, 128), F32),
            pltpu.VMEM((2, 1024, 128), F32),
            pltpu.VMEM((2, 1024, 128), F32),
            pltpu.VMEM((128, 8, 128), BF16),
            pltpu.VMEM((128, 8, 128), BF16),
            pltpu.VMEM((2, 128, 8, 128), BF16),
            pltpu.VMEM((2, 128, 8, 128), BF16),
            pltpu.VMEM((128, 8, 128), BF16),
            pltpu.VMEM((512, 512), BF16),
            pltpu.VMEM((256, 512), BF16),
            pltpu.VMEM((128, 8, 128), BF16),
            pltpu.VMEM((128, 8, 128), BF16),
            pltpu.VMEM((1024, 128), F32),
            pltpu.VMEM((1024, 128), F32),
        ] + [pltpu.SemaphoreType.DMA(())] + [pltpu.SemaphoreType.DMA((2,))] + [pltpu.SemaphoreType.DMA(())] * 6,
        compiler_params=pltpu.CompilerParams(
            collective_id=0, has_side_effects=True, vmem_limit_bytes=40 * 1024 * 1024,
        ),
        name="triangle",
    )(
        *(pltpu.with_memory_space_constraint(a, pltpu.HBM) for a in (pair, pair_mask.T, norm_gain.reshape(1, 128), left_weight, right_weight, gate_weight,
        out_gain.reshape(1, 128), out_weight))
    )


def solution(mesh):
    in_specs = (P("row", "col", None), P("row", "col"), P(), P(), P(), P(), P(), P())
    out_specs = P("row", "col", None)
    return jax.shard_map(body, mesh=mesh, in_specs=in_specs, out_specs=out_specs, check_vma=False)
```

time: 42.1 us -> 37.1 us (0.88)
  Pallas kernels: 40.4 us -> 36.3 us
  local copies, waits for them, and re-layouts: 1.67 us -> 0.71 us
    pallas_call x1, Pallas kernels: 40.4 us -> 36.3 us  [body(): pl.pallas_call(kernel, out_shape=pltpu.VMEM((64, 16, 128), BF16), in_spec...]
    unnamed x1, local copies, waits for them, and re-layouts: 1.67 us -> 0.71 us
where the time goes in v4:
time: 37.1 us; the launch traced here: 37 us
  Pallas kernels  36.3 us (98%)
  local copies, waits for them, and re-layouts  0.71 us (2%)
    pallas_call x1, Pallas kernels, body(): pl.pallas_call(kernel, out_shape=pltpu.VMEM((64, 16, 128), BF16), in_spec...  36.3 us

profile of v4, /device:TPU:1, one launch (start us, length us, event | category | flops | bytes accessed | tf_op | source)
XLA Modules:
  0.0 37.0 jit_solution(2243560205087535860)
XLA Ops:
  0.0 36.3 %triangle.1 = bf16[64,16,128]{2,1,0:T(8,128)(2,1)S(1)} custom-call(f32[64,16,128]{2,1,0:T(8,128)} %pair_hbm.1, s32[16,64]{1,0:T(8,128)} %bitcast.3, f32[1,128]{1,0:T(1,128)} %bitcast.4, bf16[128,256]{1,0:T(8,128)(2,1)} %left_w_hbm.1, bf16[128,256]{1,0:T(8,128)(2,1)} %right_w_hbm.1, bf16[128,128]{1,0:T(8,128)(2,1)} %gate_w_hbm.1, f32[1,128]{1,0:T(1,128)} %bitcast.5, ...), custom_call_target="tpu_custom_call" | custom-call | tf_op jit(solution)/shard_map/triangle/pallas_call | solution.py:196
  36.3 0.7 %copy.10 = bf16[64,16,128]{2,1,0:T(8,128)(2,1)} copy(bf16[64,16,128]{2,1,0:T(8,128)(2,1)S(1)} %triangle.1) | data formatting | bytes 524288

commit v5 on v4

--- a/solution.py
+++ b/solution.py
@@ -16,10 +16,13 @@
     return min(dz, 8 - dz) + min(dy, 4 - dy) + min(dx, 4 - dx)
 
 
-OFFSETS = sorted(
-    ((dz, dy, dx) for dx in range(4) for dy in range(4) for dz in range(8) if dz or dy or dx),
-    key=lambda offset: -hops(offset),
-)
+def offsets(weight):
+    every = [(dz, dy, dx) for dx in range(4) for dy in range(4) for dz in range(8) if dz or dy or dx]
+    along_z = lambda offset: min(offset[0], 8 - offset[0])
+    return sorted(every, key=lambda offset: (-hops(offset) + (1 - weight) * along_z(offset), along_z(offset)))
+
+
+LEFT_ORDER, RIGHT_ORDER, BACK_ORDER = offsets(0.5), offsets(1), offsets(0.5)
 MESH = pl.DeviceIdType.MESH
 
 
@@ -71,7 +74,7 @@
 
     barrier = pltpu.get_barrier_semaphore()
 
-    for offset in OFFSETS:
+    for offset in BACK_ORDER:
         pl.semaphore_signal(barrier, inc=1, device_id=peer(offset)[1], device_id_type=MESH)
     pl.semaphore_signal(barrier, inc=1, device_id=partner, device_id_type=MESH)
 
@@ -105,9 +108,9 @@
 
     pl.semaphore_wait(barrier, CHIPS)
 
-    def scatter(source, target, sem):
+    def scatter(source, target, sem, order):
         pltpu.make_async_copy(source.at[me], target.at[me], sem).start()
-        for offset in OFFSETS:
+        for offset in order:
             there, device = peer(offset)
             pltpu.make_async_remote_copy(
                 src_ref=source.at[there], dst_ref=target.at[me], send_sem=send_sem, recv_sem=sem,
@@ -119,12 +122,12 @@
         device_id=partner, device_id_type=MESH,
     )
     mix.start()
-    scatter(send_left, recv.at[0], recv_sem.at[0])
+    scatter(send_left, recv.at[0], recv_sem.at[0], LEFT_ORDER)
     mix.wait_recv()
     mine = lax.broadcasted_iota(jnp.int32, (1024, 128), 1) // 64 == core
     theirs = pltpu.roll(mixed[1].astype(F32).reshape(1024, 128), 64, 1)
     send_right[...] = jnp.where(mine, mixed[0].astype(F32).reshape(1024, 128), theirs).reshape(128, 8, 128).astype(BF16)
-    scatter(send_right, recv_right, recv_sem.at[1])
+    scatter(send_right, recv_right, recv_sem.at[1], RIGHT_ORDER)
 
     pltpu.make_async_copy(recv.at[0], recv.at[0], recv_sem.at[0]).wait()
     swap = pltpu.make_async_remote_copy(
@@ -163,7 +166,7 @@
         osend[pl.ds(quarter * 32 + 16, 16)] = uneven.reshape(16, 8, 128).astype(BF16)
 
     pltpu.make_async_copy(osend.at[me], orecv.at[me], orecv_sem).start()
-    for offset in OFFSETS:
+    for offset in BACK_ORDER:
         there, device = peer(offset)
         pltpu.make_async_remote_copy(
             src_ref=osend.at[there], dst_ref=orecv.at[me], send_sem=osend_sem, recv_sem=orecv_sem,

time: 37.1 us -> 36 us (0.970); the launches traced: 37 us -> 35.4 us
  Pallas kernels: 36.3 us -> 34.7 us
    pallas_call x1, Pallas kernels: 36.3 us -> 34.7 us  [body(): pl.pallas_call(kernel, out_shape=pltpu.VMEM((64, 16, 128), BF16), in_spec...]
where the time goes in v5:
time: 36 us; the launch traced here: 35.4 us
  Pallas kernels  34.7 us (96%)
  local copies, waits for them, and re-layouts  0.71 us (2%)
    pallas_call x1, Pallas kernels, body(): pl.pallas_call(kernel, out_shape=pltpu.VMEM((64, 16, 128), BF16), in_spec...  34.7 us

profile of v5, /device:TPU:1, one launch (start us, length us, event | category | flops | bytes accessed | tf_op | source)
XLA Modules:
  0.0 35.4 jit_solution(539208631554334818)
XLA Ops:
  0.0 34.7 %triangle.1 = bf16[64,16,128]{2,1,0:T(8,128)(2,1)S(1)} custom-call(f32[64,16,128]{2,1,0:T(8,128)} %pair_hbm.1, s32[16,64]{1,0:T(8,128)} %bitcast.3, f32[1,128]{1,0:T(1,128)} %bitcast.4, bf16[128,256]{1,0:T(8,128)(2,1)} %left_w_hbm.1, bf16[128,256]{1,0:T(8,128)(2,1)} %right_w_hbm.1, bf16[128,128]{1,0:T(8,128)(2,1)} %gate_w_hbm.1, f32[1,128]{1,0:T(1,128)} %bitcast.5, ...), custom_call_target="tpu_custom_call" | custom-call | tf_op jit(solution)/shard_map/triangle/pallas_call | solution.py:199
  34.7 0.7 %copy.10 = bf16[64,16,128]{2,1,0:T(8,128)(2,1)} copy(bf16[64,16,128]{2,1,0:T(8,128)(2,1)S(1)} %triangle.1) | data formatting | bytes 524288

commit v6 on v5

--- a/solution.py
+++ b/solution.py
@@ -74,7 +74,7 @@
 
     barrier = pltpu.get_barrier_semaphore()
 
-    for offset in BACK_ORDER:
+    for offset in RIGHT_ORDER:
         pl.semaphore_signal(barrier, inc=1, device_id=peer(offset)[1], device_id_type=MESH)
     pl.semaphore_signal(barrier, inc=1, device_id=partner, device_id_type=MESH)
 
@@ -154,16 +154,17 @@
             right[pl.ds(r * 32, 32), pl.ds(group * 128, 128)] = turned[group * 32:group * 32 + 32]
 
     low8 = lax.broadcasted_iota(jnp.int32, (128, 128), 1) < 64
-    for quarter in range(4):
-        products = jnp.dot(
-            right[...], left[:, quarter * 128:(quarter + 1) * 128], preferred_element_type=F32
-        ).reshape(16, 2, 8, 128)
-        top = products[:, 0].reshape(128, 128)
-        bottom = products[:, 1].reshape(128, 128)
-        even = jnp.where(low8, top, pltpu.roll(bottom, 64, 1))
-        uneven = jnp.where(low8, pltpu.roll(top, 64, 1), bottom)
-        osend[pl.ds(quarter * 32, 16)] = even.reshape(16, 8, 128).astype(BF16)
-        osend[pl.ds(quarter * 32 + 16, 16)] = uneven.reshape(16, 8, 128).astype(BF16)
+    for half in range(2):
+        products = jnp.dot(right[...], left[:, half * 256:(half + 1) * 256], preferred_element_type=F32)
+        for pair_at in range(2):
+            at = half * 64 + pair_at * 32
+            blocks = products[:, pair_at * 128:(pair_at + 1) * 128].reshape(16, 2, 8, 128)
+            top = blocks[:, 0].reshape(128, 128)
+            bottom = blocks[:, 1].reshape(128, 128)
+            even = jnp.where(low8, top, pltpu.roll(bottom, 64, 1))
+            uneven = jnp.where(low8, pltpu.roll(top, 64, 1), bottom)
+            osend[pl.ds(at, 16)] = even.reshape(16, 8, 128).astype(BF16)
+            osend[pl.ds(at + 16, 16)] = uneven.reshape(16, 8, 128).astype(BF16)
 
     pltpu.make_async_copy(osend.at[me], orecv.at[me], orecv_sem).start()
     for offset in BACK_ORDER:

time: 36 us -> 35.8 us (level)
  no operation moved by 1% of the time
where the time goes in v6:
time: 35.8 us; the launch traced here: 35.5 us
  Pallas kernels  34.8 us (97%)
  local copies, waits for them, and re-layouts  0.71 us (2%)
    pallas_call x1, Pallas kernels, body(): pl.pallas_call(kernel, out_shape=pltpu.VMEM((64, 16, 128), BF16), in_spec...  34.8 us

profile of v6, /device:TPU:1, one launch (start us, length us, event | category | flops | bytes accessed | tf_op | source)
XLA Modules:
  0.0 35.5 jit_solution(13901377572079890883)
XLA Ops:
  0.0 34.8 %triangle.1 = bf16[64,16,128]{2,1,0:T(8,128)(2,1)S(1)} custom-call(f32[64,16,128]{2,1,0:T(8,128)} %pair_hbm.1, s32[16,64]{1,0:T(8,128)} %bitcast.3, f32[1,128]{1,0:T(1,128)} %bitcast.4, bf16[128,256]{1,0:T(8,128)(2,1)} %left_w_hbm.1, bf16[128,256]{1,0:T(8,128)(2,1)} %right_w_hbm.1, bf16[128,128]{1,0:T(8,128)(2,1)} %gate_w_hbm.1, f32[1,128]{1,0:T(1,128)} %bitcast.5, ...), custom_call_target="tpu_custom_call" | custom-call | tf_op jit(solution)/shard_map/triangle/pallas_call | solution.py:200
  34.8 0.7 %copy.10 = bf16[64,16,128]{2,1,0:T(8,128)(2,1)} copy(bf16[64,16,128]{2,1,0:T(8,128)(2,1)S(1)} %triangle.1) | data formatting | bytes 524288

commit v7 on v6

--- a/solution.py
+++ b/solution.py
@@ -186,11 +186,13 @@
     spread = jnp.sum(centered * centered, axis=0, keepdims=True) * (1.0 / 128)
     flat[...] = (centered * lax.rsqrt(spread + EPS)).reshape(1024, 128)
     out_gain = out_gain_ref[...]
+    normed = jnp.concatenate(
+        [(flat[pl.ds(s, 128, stride=8), :].T * out_gain).astype(BF16) for s in range(8)], axis=0
+    )
+    proj = jnp.dot(normed, out_w_ref[...], preferred_element_type=F32)
     for s in range(8):
-        normed = (flat[pl.ds(s, 128, stride=8), :].T * out_gain).astype(BF16)
-        proj = jnp.dot(normed, out_w_ref[...], preferred_element_type=F32)
-        rows_out[pl.ds(s, 64, stride=16), :] = proj[:64]
-        rows_out[pl.ds(8 + s, 64, stride=16), :] = proj[64:]
+        rows_out[pl.ds(s, 64, stride=16), :] = proj[s * 128:s * 128 + 64]
+        rows_out[pl.ds(8 + s, 64, stride=16), :] = proj[s * 128 + 64:s * 128 + 128]
     out_ref[...] = (gate[...] * rows_out[...]).astype(BF16).reshape(64, 16, 128)
     pltpu.make_async_copy(osend.at[pl.ds(0, CHIPS - 1)], osend.at[pl.ds(0, CHIPS - 1)], osend_sem).wait()
 

time: 35.8 us -> 35.9 us (level)
  no operation moved by 1% of the time
where the time goes in v7:
time: 35.9 us; the launch traced here: 35.6 us
  Pallas kernels  34.9 us (97%)
  local copies, waits for them, and re-layouts  0.71 us (2%)
    pallas_call x1, Pallas kernels, body(): pl.pallas_call(kernel, out_shape=pltpu.VMEM((64, 16, 128), BF16), in_spec...  34.9 us

profile of v7, /device:TPU:1, one launch (start us, length us, event | category | flops | bytes accessed | tf_op | source)
XLA Modules:
  0.0 35.6 jit_solution(3489467983947480440)
XLA Ops:
  0.0 34.9 %triangle.1 = bf16[64,16,128]{2,1,0:T(8,128)(2,1)S(1)} custom-call(f32[64,16,128]{2,1,0:T(8,128)} %pair_hbm.1, s32[16,64]{1,0:T(8,128)} %bitcast.3, f32[1,128]{1,0:T(1,128)} %bitcast.4, bf16[128,256]{1,0:T(8,128)(2,1)} %left_w_hbm.1, bf16[128,256]{1,0:T(8,128)(2,1)} %right_w_hbm.1, bf16[128,128]{1,0:T(8,128)(2,1)} %gate_w_hbm.1, f32[1,128]{1,0:T(1,128)} %bitcast.5, ...), custom_call_target="tpu_custom_call" | custom-call | tf_op jit(solution)/shard_map/triangle/pallas_call | solution.py:202
  34.9 0.7 %copy.10 = bf16[64,16,128]{2,1,0:T(8,128)(2,1)} copy(bf16[64,16,128]{2,1,0:T(8,128)(2,1)S(1)} %triangle.1) | data formatting | bytes 524288
